TPU v7x, 512 devices: a whole 4x8x8 slice. The times are simulated.
512 devices in a mesh: area: 128 (over z, y, core), nrn: 4 (over x).
Axes of the slice: x: 4, y: 8, z: 8, core: 2. Of those that a mesh axis runs over, the one named last changes fastest.
Arguments:
- history: float32 [4, 65536, 128], P(None, ('area', 'nrn')), may hold values from -1 to 1
- drive: float32 [65536, 128], P(('area', 'nrn')), may hold values from -6 to 6
- leak: float32 [65536], P(('area', 'nrn')), may hold values from 0.1 to 0.9
- w_local: float32 [65536, 512], P(('area', 'nrn')), may hold values from -0.25 to 0.25
- w_long: float32 [65536, 4, 1152], P(('area', 'nrn')), may hold values from -0.1875 to 0.1875
- sender_rows: int32 [512, 128, 9], P(('area', 'nrn')), may hold values from 0 to 127
- delays: int32 [128, 128], P('area'), may hold values from 1 to 4
- area_sizes: int32 [128], P('area'), may hold values from 256 to 512, as said below
Outputs:
- rates: float32 [65536, 128], P(('area', 'nrn'))
Inputs may be any that keep to these rules, and one draw needn't show every extreme that they name: `area_sizes`: every area has at least half of its 512 slots live; some area has all of them live, some exactly half. `sender_rows`: indices may repeat.
All inputs are finite; a program needn't handle non-finite values.
Results may differ from a plain program's by a relative error of at most 0.0018.
Values may be sent and summed in bfloat16 or wider, within the bound.
A program may use at most 64 MiB of HBM per device.

v0:
```python
import jax
import jax.numpy as jnp
from jax import lax
from jax.sharding import PartitionSpec as P

STEPS = 6


def cut_along(x, dim, peers):
    lengths = x.shape
    pieces = x.reshape(*lengths[:dim], peers, lengths[dim] // peers, *lengths[dim + 1 :])
    return jnp.moveaxis(pieces, dim, 0)


def sum_at_owner(x, axis, dim):
    peers = lax.axis_size(axis)
    pieces = lax.all_to_all(cut_along(x, dim, peers), axis, 0, 0, tiled=True)
    return jnp.sum(pieces, axis=0)


def unround(values):
    return lax.optimization_barrier(values).astype(jnp.float32)


def local(history, drive, leak, w_local, w_long, sender_rows, delays, area_sizes):
    history_depth, block_rows, stimuli = history.shape
    nrn_count = lax.axis_size("nrn")
    area_count = sender_rows.shape[1]
    proj_count = sender_rows.shape[2]
    offsets = lax.axis_index("nrn") * block_rows + jnp.arange(block_rows, dtype=jnp.int32)
    active = (offsets < area_sizes[0]).astype(jnp.float32)[:, None]
    states = history * active[None]
    picked = ((delays[0] - 1)[:, None] * block_rows + sender_rows[0]).reshape(-1)
    grouped = lax.all_to_all(w_long, "nrn", split_axis=1, concat_axis=0, tiled=True).reshape(
        nrn_count * block_rows, -1
    )
    for iteration in range(STEPS):
        flat_states = states.reshape(history_depth * block_rows, stimuli)
        outgoing = flat_states[picked].astype(jnp.bfloat16).reshape(area_count, proj_count, stimuli)
        incoming = lax.all_to_all(outgoing, "area", split_axis=0, concat_axis=0, tiled=True)
        current = states[0].astype(jnp.bfloat16)
        local_all = lax.all_gather(current, "nrn", axis=0, tiled=True)
        sources = unround(incoming).reshape(-1, stimuli)
        long_term = sum_at_owner(
            jnp.dot(
                grouped,
                sources,
                precision=lax.Precision.HIGHEST,
                preferred_element_type=jnp.float32,
            ),
            "nrn",
            0,
        )
        inputs = (
            long_term
            + jnp.dot(
                w_local,
                unround(local_all),
                precision=lax.Precision.HIGHEST,
                preferred_element_type=jnp.float32,
            )
            + drive
        )
        updated = active * (states[0] + leak[:, None] * (jnp.tanh(inputs) - states[0]))
        states = jnp.concatenate([updated[None], states[:-1]], axis=0)
    return states[0]


def solution(mesh):
    placed = (
        P(None, ("area", "nrn"), None),
        P(("area", "nrn"), None),
        P(("area", "nrn")),
        P(("area", "nrn"), None),
        P(("area", "nrn"), None, None),
        P(("area", "nrn"), None, None),
        P("area", None),
        P("area"),
    )
    return jax.shard_map(
        local, mesh=mesh, in_specs=placed, out_specs=P(("area", "nrn"), None), check_vma=False
    )
```

profile of v0, /device:TPU:8, one launch (start us, length us, event | category | flops | bytes accessed | tf_op | source)
XLA Modules:
  0.0 353.5 jit_solution(10322337798542457753)
XLA Ops:
  0.7 0.7 multiply_bitcast_fusion
  1.4 0.2 add.110
  1.7 0.8 copy.13
  2.5 0.2 squeeze.14
  2.7 1.0 broadcast_multiply_fusion
  3.8 2.5 gather_fusion
  6.3 0.9 convert_element_type.85
  7.2 17.4 %all-to-all-start = ((bf16[128,9,128]{2,1,0:T(8,128)(2,1)}), bf16[128,9,128]{2,1,0:T(8,128)(2,1)S(1)}, u32[]{:S(2)}, u32[]{:S(2)}) async-start(bf16[128,9,128]{2,1,0:T(8,128)(2,1)} %convert_element_type.85), calls=%async_computation | async-start | bytes 1048576 | tf_op jit(solution)/shard_map/all_to_all | solution.py:40
  24.6 1.6 copy.14
  26.2 18.6 %all-to-all-done = bf16[128,9,128]{2,1,0:T(8,128)(2,1)S(1)} async-done(((bf16[128,9,128]{2,1,0:T(8,128)(2,1)}), bf16[128,9,128]{2,1,0:T(8,128)(2,1)S(1)}, u32[]{:S(2)}, u32[]{:S(2)}) %all-to-all-start) | async-done | bytes 294944 | tf_op jit(solution)/shard_map/all_to_all | solution.py:40
  44.8 4.3 %all-to-all-start.1 = ((f32[128,4,1152]{2,0,1:T(8,128)}), f32[128,4,1152]{2,0,1:T(8,128)S(1)}, u32[]{:S(2)}, u32[]{:S(2)}) async-start(f32[128,4,1152]{2,0,1:T(8,128)} %copy.14), calls=%async_computation.1 | async-start | bytes 4718592 | tf_op jit(solution)/shard_map/all_to_all | solution.py:34
  49.1 0.7 slice.39
  49.7 0.9 reshape.130
  50.6 27.7 %all-to-all-done.1 = f32[128,4,1152]{2,0,1:T(8,128)S(1)} async-done(((f32[128,4,1152]{2,0,1:T(8,128)}), f32[128,4,1152]{2,0,1:T(8,128)S(1)}, u32[]{:S(2)}, u32[]{:S(2)}) %all-to-all-start.1) | async-done | bytes 2359328 | tf_op jit(solution)/shard_map/all_to_all | solution.py:34
  78.3 2.4 convolution_bitcast_fusion.5
  80.8 0.7 copy.58
  81.5 3.4 all-to-all-start.2
  84.9 13.0 %all_gather.18 = bf16[512,128]{1,0:T(8,128)(2,1)S(1)} all-gather(bf16[128,128]{1,0:T(8,128)(2,1)S(1)} %fusion.46), channel_id=1, replica_groups=mesh['area'=128,'nrn'=4] {'nrn'}, dimensions={0}, use_global_device_ids=true | all-gather | bytes 163840 | tf_op jit(solution)/shard_map/all_gather | solution.py:42
  98.1 0.3 fusion.48
  98.4 0.6 copy-done.3
  99.0 2.9 gather_fusion.1
  102.0 27.2 %all_to_all.75 = bf16[128,9,128]{2,1,0:T(8,128)(2,1)} all-to-all(bf16[128,9,128]{2,1,0:T(8,128)(2,1)S(1)} %convert_element_type.88), channel_id=1, replica_groups=mesh['area'=128,'nrn'=4] {'area'}, dimensions={0} | all-to-all | bytes 589824 | tf_op jit(solution)/shard_map/all_to_all | solution.py:40
  129.2 1.2 reshape.134
  130.4 1.5 convolution_bitcast_fusion.4
  131.9 0.7 copy.57
  132.6 3.4 all-to-all-start.4
  136.0 13.8 %all_gather.19 = bf16[512,128]{1,0:T(8,128)(2,1)S(1)} all-gather(bf16[128,128]{1,0:T(8,128)(2,1)S(1)} %get-tuple-element.5), channel_id=1, replica_groups=mesh['area'=128,'nrn'=4] {'nrn'}, dimensions={0}, use_global_device_ids=true | all-gather | bytes 163840 | tf_op jit(solution)/shard_map/all_gather | solution.py:42
  150.0 0.3 fusion.49
  150.5 0.4 copy-done.5
  150.9 2.9 gather_fusion.2
  154.0 25.9 %all_to_all.76 = bf16[128,9,128]{2,1,0:T(8,128)(2,1)} all-to-all(bf16[128,9,128]{2,1,0:T(8,128)(2,1)S(1)} %convert_element_type.91), channel_id=1, replica_groups=mesh['area'=128,'nrn'=4] {'area'}, dimensions={0} | all-to-all | bytes 589824 | tf_op jit(solution)/shard_map/all_to_all | solution.py:40
  179.9 1.2 reshape.137
  181.1 1.5 convolution_bitcast_fusion.3
  182.6 0.7 copy.56
  183.3 3.4 all-to-all-start.6
  186.7 13.8 %all_gather.20 = bf16[512,128]{1,0:T(8,128)(2,1)S(1)} all-gather(bf16[128,128]{1,0:T(8,128)(2,1)S(1)} %get-tuple-element.7), channel_id=1, replica_groups=mesh['area'=128,'nrn'=4] {'nrn'}, dimensions={0}, use_global_device_ids=true | all-gather | bytes 163840 | tf_op jit(solution)/shard_map/all_gather | solution.py:42
  200.7 0.3 fusion.50
  201.2 0.4 copy-done.7
  201.6 2.9 gather_fusion.3
  204.6 25.9 %all_to_all.77 = bf16[128,9,128]{2,1,0:T(8,128)(2,1)} all-to-all(bf16[128,9,128]{2,1,0:T(8,128)(2,1)S(1)} %convert_element_type.94), channel_id=1, replica_groups=mesh['area'=128,'nrn'=4] {'area'}, dimensions={0} | all-to-all | bytes 589824 | tf_op jit(solution)/shard_map/all_to_all | solution.py:40
  230.6 1.2 reshape.140
  231.8 1.5 convolution_bitcast_fusion.2
  233.3 0.7 copy.55
  234.0 3.4 all-to-all-start.8
  237.4 13.8 %all_gather.21 = bf16[512,128]{1,0:T(8,128)(2,1)S(1)} all-gather(bf16[128,128]{1,0:T(8,128)(2,1)S(1)} %get-tuple-element.9), channel_id=1, replica_groups=mesh['area'=128,'nrn'=4] {'nrn'}, dimensions={0}, use_global_device_ids=true | all-gather | bytes 163840 | tf_op jit(solution)/shard_map/all_gather | solution.py:42
  251.4 0.3 fusion.51
  251.8 0.4 copy-done.9
  252.3 2.9 gather_fusion.4
  255.3 25.9 %all_to_all.78 = bf16[128,9,128]{2,1,0:T(8,128)(2,1)} all-to-all(bf16[128,9,128]{2,1,0:T(8,128)(2,1)S(1)} %convert_element_type.97), channel_id=1, replica_groups=mesh['area'=128,'nrn'=4] {'area'}, dimensions={0} | all-to-all | bytes 589824 | tf_op jit(solution)/shard_map/all_to_all | solution.py:40
  281.3 1.2 reshape.143
  282.5 1.5 convolution_bitcast_fusion.1
  283.9 0.7 copy.54
  284.7 3.4 all-to-all-start.10
  288.1 13.7 %all_gather.22 = bf16[512,128]{1,0:T(8,128)(2,1)S(1)} all-gather(bf16[128,128]{1,0:T(8,128)(2,1)S(1)} %get-tuple-element.11), channel_id=1, replica_groups=mesh['area'=128,'nrn'=4] {'nrn'}, dimensions={0}, use_global_device_ids=true | all-gather | bytes 163840 | tf_op jit(solution)/shard_map/all_gather | solution.py:42
  302.0 0.3 fusion.52
  302.3 0.6 copy-done.19
  302.9 2.9 gather_fusion.5
  305.9 25.9 %all_to_all.79 = bf16[128,9,128]{2,1,0:T(8,128)(2,1)} all-to-all(bf16[128,9,128]{2,1,0:T(8,128)(2,1)S(1)} %convert_element_type.100), channel_id=1, replica_groups=mesh['area'=128,'nrn'=4] {'area'}, dimensions={0} | all-to-all | bytes 589824 | tf_op jit(solution)/shard_map/all_to_all | solution.py:40
  331.8 1.2 reshape.146
  333.0 1.5 convolution_bitcast_fusion
  334.5 0.7 copy.53
  335.2 3.4 all-to-all-start.12
  338.6 13.8 %all_gather.23 = bf16[512,128]{1,0:T(8,128)(2,1)S(1)} all-gather(bf16[128,128]{1,0:T(8,128)(2,1)S(1)} %get-tuple-element.13), channel_id=1, replica_groups=mesh['area'=128,'nrn'=4] {'nrn'}, dimensions={0}, use_global_device_ids=true | all-gather | bytes 163840 | tf_op jit(solution)/shard_map/all_gather | solution.py:42
  352.6 0.9 fusion.41
  (76 shorter events, 2.1 us)
Async XLA Ops:
  0.0 98.0 %copy-start = (f32[128,512]{1,0:T(8,128)S(1)}, f32[128,512]{1,0:T(8,128)}, u32[]{:S(2)}) copy-start(f32[128,512]{1,0:T(8,128)} %param.11) | copy-start | bytes 786436
  3.8 20.8 %copy-start.1 = (f32[128,4,1152]{2,1,0:T(4,128)S(1)}, f32[128,4,1152]{2,1,0:T(4,128)}, u32[]{:S(2)}) copy-start(f32[128,4,1152]{2,1,0:T(4,128)} %param.12) | copy-start | bytes 7077892
  7.2 37.6 %all-to-all-start = ((bf16[128,9,128]{2,1,0:T(8,128)(2,1)}), bf16[128,9,128]{2,1,0:T(8,128)(2,1)S(1)}, u32[]{:S(2)}, u32[]{:S(2)}) async-start(bf16[128,9,128]{2,1,0:T(8,128)(2,1)} %convert_element_type.85), calls=%async_computation | async-start | bytes 1048576 | tf_op jit(solution)/shard_map/all_to_all | solution.py:40
  44.8 33.5 %all-to-all-start.1 = ((f32[128,4,1152]{2,0,1:T(8,128)}), f32[128,4,1152]{2,0,1:T(8,128)S(1)}, u32[]{:S(2)}, u32[]{:S(2)}) async-start(f32[128,4,1152]{2,0,1:T(8,128)} %copy.14), calls=%async_computation.1 | async-start | bytes 4718592 | tf_op jit(solution)/shard_map/all_to_all | solution.py:34
  50.6 47.4 %copy-start.2 = (f32[128,128]{1,0:T(8,128)S(1)}, f32[128,128]{1,0:T(8,128)}, u32[]{:S(2)}) copy-start(f32[128,128]{1,0:T(8,128)} %param.9) | copy-start | bytes 196612
  50.6 47.4 %copy-start.21 = (f32[128]{0:T(128)S(1)}, f32[128]{0:T(128)}, u32[]{:S(2)}) copy-start(f32[128]{0:T(128)} %param.10) | copy-start | bytes 1540
  78.3 20.0 %copy-start.11 = (bf16[3,128,128]{2,1,0:T(8,128)(2,1)S(1)}, bf16[3,128,128]{2,1,0:T(8,128)(2,1)}, u32[]{:S(2)}) copy-start(bf16[3,128,128]{2,1,0:T(8,128)(2,1)} %slice.39) | copy-start | bytes 294916
  81.5 16.4 %all-to-all-start.2 = ((f32[4,128,128]{1,2,0:T(8,128)}), f32[4,128,128]{1,2,0:T(8,128)S(1)}, u32[]{:S(2)}, u32[]{:S(2)}) async-start(f32[4,128,128]{1,2,0:T(8,128)} %bitcast.180), calls=%async_computation.2 | async-start | bytes 524288 | tf_op jit(solution)/shard_map/all_to_all | solution.py:17
  98.3 0.6 copy-start.3
  129.2 20.6 %copy-start.4 = (f32[128,128]{1,0:T(8,128)S(1)}, f32[128,128]{1,0:T(8,128)}, u32[]{:S(2)}) copy-start(f32[128,128]{1,0:T(8,128)} %copy-done.3) | copy-start | bytes 196612
  129.2 20.6 %copy-start.12 = (bf16[3,128,128]{2,1,0:T(8,128)(2,1)S(1)}, bf16[3,128,128]{2,1,0:T(8,128)(2,1)}, u32[]{:S(2)}) copy-start(bf16[3,128,128]{2,1,0:T(8,128)(2,1)} %slice.39) | copy-start | bytes 294916
  132.6 17.3 %all-to-all-start.4 = ((f32[4,128,128]{1,2,0:T(8,128)}), f32[4,128,128]{1,2,0:T(8,128)S(1)}, u32[]{:S(2)}, u32[]{:S(2)}) async-start(f32[4,128,128]{1,2,0:T(8,128)} %bitcast.179), calls=%async_computation.4 | async-start | bytes 524288 | tf_op jit(solution)/shard_map/all_to_all | solution.py:17
  149.8 0.6 copy-start.13
  150.3 0.6 copy-start.5
  179.9 20.6 %copy-start.6 = (f32[128,128]{1,0:T(8,128)S(1)}, f32[128,128]{1,0:T(8,128)}, u32[]{:S(2)}) copy-start(f32[128,128]{1,0:T(8,128)} %copy-done.5) | copy-start | bytes 196612
  179.9 20.6 %copy-start.14 = (bf16[3,128,128]{2,1,0:T(8,128)(2,1)S(1)}, bf16[3,128,128]{2,1,0:T(8,128)(2,1)}, u32[]{:S(2)}) copy-start(bf16[3,128,128]{2,1,0:T(8,128)(2,1)} %copy-done.13) | copy-start | bytes 294916
  183.3 17.2 %all-to-all-start.6 = ((f32[4,128,128]{1,2,0:T(8,128)}), f32[4,128,128]{1,2,0:T(8,128)S(1)}, u32[]{:S(2)}, u32[]{:S(2)}) async-start(f32[4,128,128]{1,2,0:T(8,128)} %bitcast.178), calls=%async_computation.6 | async-start | bytes 524288 | tf_op jit(solution)/shard_map/all_to_all | solution.py:17
  200.5 0.6 copy-start.15
  200.9 0.6 copy-start.7
  230.6 20.6 %copy-start.8 = (f32[128,128]{1,0:T(8,128)S(1)}, f32[128,128]{1,0:T(8,128)}, u32[]{:S(2)}) copy-start(f32[128,128]{1,0:T(8,128)} %copy-done.7) | copy-start | bytes 196612
  230.6 20.6 %copy-start.16 = (bf16[3,128,128]{2,1,0:T(8,128)(2,1)S(1)}, bf16[3,128,128]{2,1,0:T(8,128)(2,1)}, u32[]{:S(2)}) copy-start(bf16[3,128,128]{2,1,0:T(8,128)(2,1)} %copy-done.15) | copy-start | bytes 294916
  234.0 17.2 %all-to-all-start.8 = ((f32[4,128,128]{1,2,0:T(8,128)}), f32[4,128,128]{1,2,0:T(8,128)S(1)}, u32[]{:S(2)}, u32[]{:S(2)}) async-start(f32[4,128,128]{1,2,0:T(8,128)} %bitcast.177), calls=%async_computation.8 | async-start | bytes 524288 | tf_op jit(solution)/shard_map/all_to_all | solution.py:17
  251.2 0.6 copy-start.17
  251.6 0.6 copy-start.9
  281.3 20.5 %copy-start.10 = (f32[128,128]{1,0:T(8,128)S(1)}, f32[128,128]{1,0:T(8,128)}, u32[]{:S(2)}) copy-start(f32[128,128]{1,0:T(8,128)} %copy-done.9) | copy-start | bytes 196612
  281.3 20.5 %copy-start.18 = (bf16[3,128,128]{2,1,0:T(8,128)(2,1)S(1)}, bf16[3,128,128]{2,1,0:T(8,128)(2,1)}, u32[]{:S(2)}) copy-start(bf16[3,128,128]{2,1,0:T(8,128)(2,1)} %copy-done.17) | copy-start | bytes 294916
  284.7 17.2 %all-to-all-start.10 = ((f32[4,128,128]{1,2,0:T(8,128)}), f32[4,128,128]{1,2,0:T(8,128)S(1)}, u32[]{:S(2)}, u32[]{:S(2)}) async-start(f32[4,128,128]{1,2,0:T(8,128)} %bitcast.176), calls=%async_computation.10 | async-start | bytes 524288 | tf_op jit(solution)/shard_map/all_to_all | solution.py:17
  302.2 0.6 copy-start.19
  333.0 19.5 %copy-start.20 = (f32[128,128]{1,0:T(8,128)S(1)}, f32[128,128]{1,0:T(8,128)}, u32[]{:S(2)}) copy-start(f32[128,128]{1,0:T(8,128)} %copy-done.19) | copy-start | bytes 196612
  335.2 17.2 %all-to-all-start.12 = ((f32[4,128,128]{1,2,0:T(8,128)}), f32[4,128,128]{1,2,0:T(8,128)S(1)}, u32[]{:S(2)}, u32[]{:S(2)}) async-start(f32[4,128,128]{1,2,0:T(8,128)} %bitcast.175), calls=%async_computation.12 | async-start | bytes 524288 | tf_op jit(solution)/shard_map/all_to_all | solution.py:17
where the time goes:
time: 355 us; the launch traced here: 353 us
  blocking collectives  213 us (60%)
  waiting for transfers between devices  46.3 us (13%)
  starting transfers between devices  42.1 us (12%)
  local copies, waits for them, and re-layouts  37 us (10%)
  matrix products  12 us (3%)
    all_to_all x5, blocking collectives, local(): lax.all_to_all(outgoing, 'area', split_axis=0, concat_axis=0, tiled=True)  131 us
    all_gather x6, blocking collectives, local(): local_all = lax.all_gather(current, 'nrn', axis=0, tiled=True)  81.9 us
    all_to_all x1, waiting for transfers between devices, local(): lax.all_to_all(w_long, 'nrn', split_axis=1, concat_axis=0, tiled=True)  27.7 us
    all_to_all x6, starting transfers between devices, sum_at_owner(): pieces = lax.all_to_all(cut_along(x, dim, peers), axis, 0, 0, tiled=True)  20.4 us
    all_to_all x1, waiting for transfers between devices, local(): lax.all_to_all(outgoing, 'area', split_axis=0, concat_axis=0, tiled=True)  18.6 us
    all_to_all x1, starting transfers between devices, local(): lax.all_to_all(outgoing, 'area', split_axis=0, concat_axis=0, tiled=True)  17.4 us
    gather x6, local copies, waits for them, and re-layouts, local(): flat_states[picked].astype(jnp.bfloat16)  17.1 us
    dot_general x6, matrix products, local(): jnp.dot(grouped, sources, precision=lax.Precision.HIGHEST, preferred_elem...  9.74 us
  transfers between devices with their start and end apart: 8, of which 2 were waited for; matrix products, arithmetic and copies ran while one was open for 1% of the time, Pallas kernels for 0%

commit v1 on v0

--- a/solution.py
+++ b/solution.py
@@ -39,7 +39,9 @@
         outgoing = flat_states[picked].astype(jnp.bfloat16).reshape(area_count, proj_count, stimuli)
         incoming = lax.all_to_all(outgoing, "area", split_axis=0, concat_axis=0, tiled=True)
         current = states[0].astype(jnp.bfloat16)
-        local_all = lax.all_gather(current, "nrn", axis=0, tiled=True)
+        local_all = jnp.concatenate(
+            lax.all_to_all(jnp.stack([current] * lax.axis_size("nrn")), "nrn", 0, 0), axis=0
+        )
         sources = unround(incoming).reshape(-1, stimuli)
         long_term = sum_at_owner(
             jnp.dot(

time: 355 us -> 369 us (1.039)
  the two profiles are of different devices: /device:TPU:8 before, /device:TPU:1 now
where the time goes in v1:
time: 369 us; the launch traced here: 367 us
  blocking collectives  140 us (38%)
  waiting for transfers between devices  102 us (28%)
  starting transfers between devices  66.1 us (18%)
  local copies, waits for them, and re-layouts  39 us (11%)
  matrix products  16.5 us (4%)
    all_to_all x5, blocking collectives, local(): lax.all_to_all(outgoing, 'area', split_axis=0, concat_axis=0, tiled=True)  140 us
    all_to_all x6, waiting for transfers between devices, sum_at_owner(): pieces = lax.all_to_all(cut_along(x, dim, peers), axis, 0, 0, tiled=True)  35.1 us
    all_to_all x1, waiting for transfers between devices, local(): lax.all_to_all(w_long, 'nrn', split_axis=1, concat_axis=0, tiled=True)  28.5 us
    all_to_all x6, starting transfers between devices, local(): lax.all_to_all(jnp.stack([current] * lax.axis_size('nrn')), 'nrn', 0, 0)  23.1 us
    all_to_all x6, starting transfers between devices, sum_at_owner(): pieces = lax.all_to_all(cut_along(x, dim, peers), axis, 0, 0, tiled=True)  20.6 us
    all_to_all x6, waiting for transfers between devices, local(): lax.all_to_all(jnp.stack([current] * lax.axis_size('nrn')), 'nrn', 0, 0)  19.1 us
    all_to_all x1, waiting for transfers between devices, local(): lax.all_to_all(outgoing, 'area', split_axis=0, concat_axis=0, tiled=True)  19 us
    all_to_all x1, starting transfers between devices, local(): lax.all_to_all(outgoing, 'area', split_axis=0, concat_axis=0, tiled=True)  18.4 us
  transfers between devices with their start and end apart: 14, of which 14 were waited for; matrix products, arithmetic and copies ran while one was open for 5% of the time, Pallas kernels for 0%

profile of v1, /device:TPU:1, one launch (start us, length us, event | category | flops | bytes accessed | tf_op | source)
XLA Modules:
  0.0 366.6 jit_solution(5924570959360936856)
XLA Ops:
  1.7 0.8 copy.13
  2.7 1.0 broadcast_multiply_fusion
  3.8 2.5 gather_fusion
  6.3 0.9 convert_element_type.86
  7.2 18.4 %all-to-all-start = ((bf16[128,9,128]{2,1,0:T(8,128)(2,1)}), bf16[128,9,128]{2,1,0:T(8,128)(2,1)S(1)}, u32[]{:S(2)}, u32[]{:S(2)}) async-start(bf16[128,9,128]{2,1,0:T(8,128)(2,1)} %convert_element_type.86), calls=%async_computation | async-start | bytes 1048576 | tf_op jit(solution)/shard_map/all_to_all | solution.py:40
  25.7 1.6 copy.14
  27.2 19.0 %all-to-all-done = bf16[128,9,128]{2,1,0:T(8,128)(2,1)S(1)} async-done(((bf16[128,9,128]{2,1,0:T(8,128)(2,1)}), bf16[128,9,128]{2,1,0:T(8,128)(2,1)S(1)}, u32[]{:S(2)}, u32[]{:S(2)}) %all-to-all-start) | async-done | bytes 294944 | tf_op jit(solution)/shard_map/all_to_all | solution.py:40
  46.2 4.0 %all-to-all-start.1 = ((f32[128,4,1152]{2,0,1:T(8,128)}), f32[128,4,1152]{2,0,1:T(8,128)S(1)}, u32[]{:S(2)}, u32[]{:S(2)}) async-start(f32[128,4,1152]{2,0,1:T(8,128)} %copy.14), calls=%async_computation.1 | async-start | bytes 4718592 | tf_op jit(solution)/shard_map/all_to_all | solution.py:34
  50.2 0.9 reshape.159
  51.1 28.5 %all-to-all-done.1 = f32[128,4,1152]{2,0,1:T(8,128)S(1)} async-done(((f32[128,4,1152]{2,0,1:T(8,128)}), f32[128,4,1152]{2,0,1:T(8,128)S(1)}, u32[]{:S(2)}, u32[]{:S(2)}) %all-to-all-start.1) | async-done | bytes 2359328 | tf_op jit(solution)/shard_map/all_to_all | solution.py:34
  80.3 3.3 all-to-all-start.3
  83.6 2.4 convolution_bitcast_fusion.5
  86.1 0.7 copy.58
  86.8 1.6 all-to-all-done.3
  88.4 3.4 all-to-all-start.2
  91.8 5.5 %all-to-all-done.2 = f32[4,128,128]{1,2,0:T(8,128)S(1)} async-done(((f32[4,128,128]{1,2,0:T(8,128)}), f32[4,128,128]{1,2,0:T(8,128)S(1)}, u32[]{:S(2)}, u32[]{:S(2)}) %all-to-all-start.2) | async-done | bytes 262176 | tf_op jit(solution)/shard_map/all_to_all | solution.py:17
  98.4 2.9 gather_fusion.1
  101.3 0.9 convert_element_type.89
  102.2 29.1 %all_to_all.105 = bf16[128,9,128]{2,1,0:T(8,128)(2,1)S(1)} all-to-all(bf16[128,9,128]{2,1,0:T(8,128)(2,1)} %convert_element_type.89), channel_id=1, replica_groups=mesh['area'=128,'nrn'=4] {'area'}, dimensions={0} | all-to-all | bytes 589824 | tf_op jit(solution)/shard_map/all_to_all | solution.py:40
  132.0 3.9 %all-to-all-start.6 = ((bf16[4,128,128]{2,1,0:T(8,128)(2,1)}), bf16[4,128,128]{2,1,0:T(8,128)(2,1)}, u32[]{:S(2)}, u32[]{:S(2)}) async-start(bf16[4,128,128]{2,1,0:T(8,128)(2,1)} %stack.16), calls=%async_computation.6 | async-start | bytes 262144 | tf_op jit(solution)/shard_map/all_to_all | solution.py:43
  136.1 1.5 convolution_bitcast_fusion.4
  137.6 0.7 copy.57
  138.3 3.5 all-to-all-done.6
  141.8 3.4 all-to-all-start.5
  145.2 6.0 %all-to-all-done.5 = f32[4,128,128]{1,2,0:T(8,128)S(1)} async-done(((f32[4,128,128]{1,2,0:T(8,128)}), f32[4,128,128]{1,2,0:T(8,128)S(1)}, u32[]{:S(2)}, u32[]{:S(2)}) %all-to-all-start.5) | async-done | bytes 262176 | tf_op jit(solution)/shard_map/all_to_all | solution.py:17
  151.3 1.2 fusion.49
  153.1 2.9 gather_fusion.2
  156.1 0.9 convert_element_type.92
  157.0 27.8 %all_to_all.106 = bf16[128,9,128]{2,1,0:T(8,128)(2,1)S(1)} all-to-all(bf16[128,9,128]{2,1,0:T(8,128)(2,1)} %convert_element_type.92), channel_id=1, replica_groups=mesh['area'=128,'nrn'=4] {'area'}, dimensions={0} | all-to-all | bytes 589824 | tf_op jit(solution)/shard_map/all_to_all | solution.py:40
  185.5 3.9 %all-to-all-start.9 = ((bf16[4,128,128]{2,1,0:T(8,128)(2,1)}), bf16[4,128,128]{2,1,0:T(8,128)(2,1)}, u32[]{:S(2)}, u32[]{:S(2)}) async-start(bf16[4,128,128]{2,1,0:T(8,128)(2,1)} %stack.17), calls=%async_computation.9 | async-start | bytes 262144 | tf_op jit(solution)/shard_map/all_to_all | solution.py:43
  189.6 1.5 convolution_bitcast_fusion.3
  191.8 3.5 all-to-all-done.9
  195.3 3.4 all-to-all-start.8
  198.7 6.0 %all-to-all-done.8 = f32[4,128,128]{1,2,0:T(8,128)S(1)} async-done(((f32[4,128,128]{1,2,0:T(8,128)}), f32[4,128,128]{1,2,0:T(8,128)S(1)}, u32[]{:S(2)}, u32[]{:S(2)}) %all-to-all-start.8) | async-done | bytes 262176 | tf_op jit(solution)/shard_map/all_to_all | solution.py:17
  204.8 1.2 fusion.50
  206.6 2.9 gather_fusion.3
  209.6 0.9 convert_element_type.95
  210.5 27.7 %all_to_all.107 = bf16[128,9,128]{2,1,0:T(8,128)(2,1)S(1)} all-to-all(bf16[128,9,128]{2,1,0:T(8,128)(2,1)} %convert_element_type.95), channel_id=1, replica_groups=mesh['area'=128,'nrn'=4] {'area'}, dimensions={0} | all-to-all | bytes 589824 | tf_op jit(solution)/shard_map/all_to_all | solution.py:40
  238.8 3.9 %all-to-all-start.12 = ((bf16[4,128,128]{2,1,0:T(8,128)(2,1)}), bf16[4,128,128]{2,1,0:T(8,128)(2,1)}, u32[]{:S(2)}, u32[]{:S(2)}) async-start(bf16[4,128,128]{2,1,0:T(8,128)(2,1)} %stack.18), calls=%async_computation.12 | async-start | bytes 262144 | tf_op jit(solution)/shard_map/all_to_all | solution.py:43
  243.0 1.5 convolution_bitcast_fusion.2
  245.1 3.5 all-to-all-done.12
  248.6 3.4 all-to-all-start.11
  252.1 6.0 %all-to-all-done.11 = f32[4,128,128]{1,2,0:T(8,128)S(1)} async-done(((f32[4,128,128]{1,2,0:T(8,128)}), f32[4,128,128]{1,2,0:T(8,128)S(1)}, u32[]{:S(2)}, u32[]{:S(2)}) %all-to-all-start.11) | async-done | bytes 262176 | tf_op jit(solution)/shard_map/all_to_all | solution.py:17
  258.2 1.2 fusion.51
  260.0 2.9 gather_fusion.4
  262.9 0.9 convert_element_type.98
  263.8 27.7 %all_to_all.108 = bf16[128,9,128]{2,1,0:T(8,128)(2,1)S(1)} all-to-all(bf16[128,9,128]{2,1,0:T(8,128)(2,1)} %convert_element_type.98), channel_id=1, replica_groups=mesh['area'=128,'nrn'=4] {'area'}, dimensions={0} | all-to-all | bytes 589824 | tf_op jit(solution)/shard_map/all_to_all | solution.py:40
  292.2 3.9 %all-to-all-start.15 = ((bf16[4,128,128]{2,1,0:T(8,128)(2,1)}), bf16[4,128,128]{2,1,0:T(8,128)(2,1)}, u32[]{:S(2)}, u32[]{:S(2)}) async-start(bf16[4,128,128]{2,1,0:T(8,128)(2,1)} %stack.19), calls=%async_computation.15 | async-start | bytes 262144 | tf_op jit(solution)/shard_map/all_to_all | solution.py:43
  296.3 1.5 convolution_bitcast_fusion.1
  297.7 0.7 copy.54
  298.5 3.5 all-to-all-done.15
  301.9 3.6 all-to-all-start.14
  305.6 5.7 %all-to-all-done.14 = f32[4,128,128]{1,2,0:T(8,128)S(1)} async-done(((f32[4,128,128]{1,2,0:T(8,128)}), f32[4,128,128]{1,2,0:T(8,128)S(1)}, u32[]{:S(2)}, u32[]{:S(2)}) %all-to-all-start.14) | async-done | bytes 262176 | tf_op jit(solution)/shard_map/all_to_all | solution.py:17
  311.5 1.2 fusion.52
  313.3 2.9 gather_fusion.5
  316.2 0.9 convert_element_type.101
  317.1 27.7 %all_to_all.109 = bf16[128,9,128]{2,1,0:T(8,128)(2,1)S(1)} all-to-all(bf16[128,9,128]{2,1,0:T(8,128)(2,1)} %convert_element_type.101), channel_id=1, replica_groups=mesh['area'=128,'nrn'=4] {'area'}, dimensions={0} | all-to-all | bytes 589824 | tf_op jit(solution)/shard_map/all_to_all | solution.py:40
  345.5 3.9 %all-to-all-start.18 = ((bf16[4,128,128]{2,1,0:T(8,128)(2,1)}), bf16[4,128,128]{2,1,0:T(8,128)(2,1)}, u32[]{:S(2)}, u32[]{:S(2)}) async-start(bf16[4,128,128]{2,1,0:T(8,128)(2,1)} %stack.20), calls=%async_computation.18 | async-start | bytes 262144 | tf_op jit(solution)/shard_map/all_to_all | solution.py:43
  349.6 1.5 convolution_bitcast_fusion
  351.1 0.7 copy.53
  351.8 3.5 all-to-all-done.18
  355.3 3.4 all-to-all-start.17
  358.7 6.0 %all-to-all-done.17 = f32[4,128,128]{1,2,0:T(8,128)S(1)} async-done(((f32[4,128,128]{1,2,0:T(8,128)}), f32[4,128,128]{1,2,0:T(8,128)S(1)}, u32[]{:S(2)}, u32[]{:S(2)}) %all-to-all-start.17) | async-done | bytes 262176 | tf_op jit(solution)/shard_map/all_to_all | solution.py:17
  364.8 1.8 fusion.41
  (88 shorter events, 11.5 us)
Async XLA Ops:
  0.0 97.4 %copy-start = (f32[128,512]{1,0:T(8,128)S(1)}, f32[128,512]{1,0:T(8,128)}, u32[]{:S(2)}) copy-start(f32[128,512]{1,0:T(8,128)} %param.11) | copy-start | bytes 786436
  3.8 21.9 %copy-start.1 = (f32[128,4,1152]{2,1,0:T(4,128)S(1)}, f32[128,4,1152]{2,1,0:T(4,128)}, u32[]{:S(2)}) copy-start(f32[128,4,1152]{2,1,0:T(4,128)} %param.12) | copy-start | bytes 7077892
  7.2 39.0 %all-to-all-start = ((bf16[128,9,128]{2,1,0:T(8,128)(2,1)}), bf16[128,9,128]{2,1,0:T(8,128)(2,1)S(1)}, u32[]{:S(2)}, u32[]{:S(2)}) async-start(bf16[128,9,128]{2,1,0:T(8,128)(2,1)} %convert_element_type.86), calls=%async_computation | async-start | bytes 1048576 | tf_op jit(solution)/shard_map/all_to_all | solution.py:40
  46.2 33.4 %all-to-all-start.1 = ((f32[128,4,1152]{2,0,1:T(8,128)}), f32[128,4,1152]{2,0,1:T(8,128)S(1)}, u32[]{:S(2)}, u32[]{:S(2)}) async-start(f32[128,4,1152]{2,0,1:T(8,128)} %copy.14), calls=%async_computation.1 | async-start | bytes 4718592 | tf_op jit(solution)/shard_map/all_to_all | solution.py:34
  80.3 8.1 %all-to-all-start.3 = ((bf16[4,128,128]{2,1,0:T(8,128)(2,1)}), bf16[4,128,128]{2,1,0:T(8,128)(2,1)S(1)}, u32[]{:S(2)}, u32[]{:S(2)}) async-start(bf16[4,128,128]{2,1,0:T(8,128)(2,1)} %stack.15), calls=%async_computation.3 | async-start | bytes 262144 | tf_op jit(solution)/shard_map/all_to_all | solution.py:43
  83.6 13.8 %copy-start.2 = (f32[128,128]{1,0:T(8,128)S(1)}, f32[128,128]{1,0:T(8,128)}, u32[]{:S(2)}) copy-start(f32[128,128]{1,0:T(8,128)} %param.9) | copy-start | bytes 196612
  83.6 13.8 %copy-start.21 = (f32[128]{0:T(128)S(1)}, f32[128]{0:T(128)}, u32[]{:S(2)}) copy-start(f32[128]{0:T(128)} %param.10) | copy-start | bytes 1540
  88.4 8.9 %all-to-all-start.2 = ((f32[4,128,128]{1,2,0:T(8,128)}), f32[4,128,128]{1,2,0:T(8,128)S(1)}, u32[]{:S(2)}, u32[]{:S(2)}) async-start(f32[4,128,128]{1,2,0:T(8,128)} %bitcast.184), calls=%async_computation.2 | async-start | bytes 524288 | tf_op jit(solution)/shard_map/all_to_all | solution.py:17
  91.8 10.4 %copy-start.11 = (bf16[3,128,128]{2,1,0:T(8,128)(2,1)}, bf16[3,128,128]{2,1,0:T(8,128)(2,1)S(1)}, u32[]{:S(2)}) copy-start(bf16[3,128,128]{2,1,0:T(8,128)(2,1)S(1)} %slice.39) | copy-start | bytes 294916
  97.7 0.6 copy-start.3
  132.0 9.8 %all-to-all-start.6 = ((bf16[4,128,128]{2,1,0:T(8,128)(2,1)}), bf16[4,128,128]{2,1,0:T(8,128)(2,1)}, u32[]{:S(2)}, u32[]{:S(2)}) async-start(bf16[4,128,128]{2,1,0:T(8,128)(2,1)} %stack.16), calls=%async_computation.6 | async-start | bytes 262144 | tf_op jit(solution)/shard_map/all_to_all | solution.py:43
  136.1 9.1 %copy-start.4 = (f32[128,128]{1,0:T(8,128)S(1)}, f32[128,128]{1,0:T(8,128)}, u32[]{:S(2)}) copy-start(f32[128,128]{1,0:T(8,128)} %copy-done.3) | copy-start | bytes 196612
  136.1 9.1 %copy-start.12 = (bf16[3,128,128]{2,1,0:T(8,128)(2,1)S(1)}, bf16[3,128,128]{2,1,0:T(8,128)(2,1)}, u32[]{:S(2)}) copy-start(bf16[3,128,128]{2,1,0:T(8,128)(2,1)} %copy-done.11) | copy-start | bytes 294916
  141.8 9.4 %all-to-all-start.5 = ((f32[4,128,128]{1,2,0:T(8,128)}), f32[4,128,128]{1,2,0:T(8,128)S(1)}, u32[]{:S(2)}, u32[]{:S(2)}) async-start(f32[4,128,128]{1,2,0:T(8,128)} %bitcast.183), calls=%async_computation.5 | async-start | bytes 524288 | tf_op jit(solution)/shard_map/all_to_all | solution.py:17
  145.2 10.8 %copy-start.13 = (bf16[3,128,128]{2,1,0:T(8,128)(2,1)}, bf16[3,128,128]{2,1,0:T(8,128)(2,1)S(1)}, u32[]{:S(2)}) copy-start(bf16[3,128,128]{2,1,0:T(8,128)(2,1)S(1)} %fusion.45) | copy-start | bytes 294916
  152.5 0.6 copy-start.5
  185.5 9.8 %all-to-all-start.9 = ((bf16[4,128,128]{2,1,0:T(8,128)(2,1)}), bf16[4,128,128]{2,1,0:T(8,128)(2,1)}, u32[]{:S(2)}, u32[]{:S(2)}) async-start(bf16[4,128,128]{2,1,0:T(8,128)(2,1)} %stack.17), calls=%async_computation.9 | async-start | bytes 262144 | tf_op jit(solution)/shard_map/all_to_all | solution.py:43
  189.6 9.1 %copy-start.6 = (f32[128,128]{1,0:T(8,128)S(1)}, f32[128,128]{1,0:T(8,128)}, u32[]{:S(2)}) copy-start(f32[128,128]{1,0:T(8,128)} %copy-done.5) | copy-start | bytes 196612
  189.6 9.1 %copy-start.14 = (bf16[3,128,128]{2,1,0:T(8,128)(2,1)S(1)}, bf16[3,128,128]{2,1,0:T(8,128)(2,1)}, u32[]{:S(2)}) copy-start(bf16[3,128,128]{2,1,0:T(8,128)(2,1)} %copy-done.13) | copy-start | bytes 294916
  195.3 9.4 %all-to-all-start.8 = ((f32[4,128,128]{1,2,0:T(8,128)}), f32[4,128,128]{1,2,0:T(8,128)S(1)}, u32[]{:S(2)}, u32[]{:S(2)}) async-start(f32[4,128,128]{1,2,0:T(8,128)} %bitcast.182), calls=%async_computation.8 | async-start | bytes 524288 | tf_op jit(solution)/shard_map/all_to_all | solution.py:17
  198.7 10.8 %copy-start.15 = (bf16[3,128,128]{2,1,0:T(8,128)(2,1)}, bf16[3,128,128]{2,1,0:T(8,128)(2,1)S(1)}, u32[]{:S(2)}) copy-start(bf16[3,128,128]{2,1,0:T(8,128)(2,1)S(1)} %fusion.44) | copy-start | bytes 294916
  206.0 0.6 copy-start.7
  238.8 9.8 %all-to-all-start.12 = ((bf16[4,128,128]{2,1,0:T(8,128)(2,1)}), bf16[4,128,128]{2,1,0:T(8,128)(2,1)}, u32[]{:S(2)}, u32[]{:S(2)}) async-start(bf16[4,128,128]{2,1,0:T(8,128)(2,1)} %stack.18), calls=%async_computation.12 | async-start | bytes 262144 | tf_op jit(solution)/shard_map/all_to_all | solution.py:43
  242.9 9.1 %copy-start.8 = (f32[128,128]{1,0:T(8,128)S(1)}, f32[128,128]{1,0:T(8,128)}, u32[]{:S(2)}) copy-start(f32[128,128]{1,0:T(8,128)} %copy-done.7) | copy-start | bytes 196612
  242.9 9.1 %copy-start.16 = (bf16[3,128,128]{2,1,0:T(8,128)(2,1)S(1)}, bf16[3,128,128]{2,1,0:T(8,128)(2,1)}, u32[]{:S(2)}) copy-start(bf16[3,128,128]{2,1,0:T(8,128)(2,1)} %copy-done.15) | copy-start | bytes 294916
  248.6 9.4 %all-to-all-start.11 = ((f32[4,128,128]{1,2,0:T(8,128)}), f32[4,128,128]{1,2,0:T(8,128)S(1)}, u32[]{:S(2)}, u32[]{:S(2)}) async-start(f32[4,128,128]{1,2,0:T(8,128)} %bitcast.181), calls=%async_computation.11 | async-start | bytes 524288 | tf_op jit(solution)/shard_map/all_to_all | solution.py:17
  252.1 10.8 %copy-start.17 = (bf16[3,128,128]{2,1,0:T(8,128)(2,1)}, bf16[3,128,128]{2,1,0:T(8,128)(2,1)S(1)}, u32[]{:S(2)}) copy-start(bf16[3,128,128]{2,1,0:T(8,128)(2,1)S(1)} %fusion.43) | copy-start | bytes 294916
  259.3 0.6 copy-start.9
  292.2 9.8 %all-to-all-start.15 = ((bf16[4,128,128]{2,1,0:T(8,128)(2,1)}), bf16[4,128,128]{2,1,0:T(8,128)(2,1)}, u32[]{:S(2)}, u32[]{:S(2)}) async-start(bf16[4,128,128]{2,1,0:T(8,128)(2,1)} %stack.19), calls=%async_computation.15 | async-start | bytes 262144 | tf_op jit(solution)/shard_map/all_to_all | solution.py:43
  296.3 9.3 %copy-start.10 = (f32[128,128]{1,0:T(8,128)S(1)}, f32[128,128]{1,0:T(8,128)}, u32[]{:S(2)}) copy-start(f32[128,128]{1,0:T(8,128)} %copy-done.9) | copy-start | bytes 196612
  296.3 9.3 %copy-start.18 = (bf16[3,128,128]{2,1,0:T(8,128)(2,1)S(1)}, bf16[3,128,128]{2,1,0:T(8,128)(2,1)}, u32[]{:S(2)}) copy-start(bf16[3,128,128]{2,1,0:T(8,128)(2,1)} %copy-done.17) | copy-start | bytes 294916
  301.9 9.4 %all-to-all-start.14 = ((f32[4,128,128]{1,2,0:T(8,128)}), f32[4,128,128]{1,2,0:T(8,128)S(1)}, u32[]{:S(2)}, u32[]{:S(2)}) async-start(f32[4,128,128]{1,2,0:T(8,128)} %bitcast.180), calls=%async_computation.14 | async-start | bytes 524288 | tf_op jit(solution)/shard_map/all_to_all | solution.py:17
  312.7 0.6 copy-start.19
  345.5 9.8 %all-to-all-start.18 = ((bf16[4,128,128]{2,1,0:T(8,128)(2,1)}), bf16[4,128,128]{2,1,0:T(8,128)(2,1)}, u32[]{:S(2)}, u32[]{:S(2)}) async-start(bf16[4,128,128]{2,1,0:T(8,128)(2,1)} %stack.20), calls=%async_computation.18 | async-start | bytes 262144 | tf_op jit(solution)/shard_map/all_to_all | solution.py:43
  349.6 15.2 %copy-start.20 = (f32[128,128]{1,0:T(8,128)S(1)}, f32[128,128]{1,0:T(8,128)}, u32[]{:S(2)}) copy-start(f32[128,128]{1,0:T(8,128)} %copy-done.19) | copy-start | bytes 196612
  355.3 9.4 %all-to-all-start.17 = ((f32[4,128,128]{1,2,0:T(8,128)}), f32[4,128,128]{1,2,0:T(8,128)S(1)}, u32[]{:S(2)}, u32[]{:S(2)}) async-start(f32[4,128,128]{1,2,0:T(8,128)} %bitcast.179), calls=%async_computation.17 | async-start | bytes 524288 | tf_op jit(solution)/shard_map/all_to_all | solution.py:17
